TPU v7x, 256 devices: a whole 4x4x8 slice. The times are simulated.
256 devices in a mesh: dp: 16 (over z, core), expert: 16 (over x, y).
Axes of the slice: x: 4, y: 4, z: 8, core: 2. Of those that a mesh axis runs over, the one named last changes fastest.
Arguments:
- attn_rows: bfloat16 [98304, 2048], P(('dp', 'expert')), may hold values from -6 to 6
- out_grad: bfloat16 [98304, 2048], P(('dp', 'expert')), may hold values from -1.5 to 1.5
- owner_rows: int32 [16, 16], P('expert'), may hold values from 1 to 384, 4096 in all within a row
- routes: int32 [65536, 1], P(('dp', 'expert')), may hold values from 0 to 15; in each aligned block of 256 rows (0 to 255, 256 to 511, ...) at most 24 rows name the same one
- gates: bfloat16 [65536], P(('dp', 'expert')), may hold values from 0.25 to 1
- gate_weight: bfloat16 [16, 2048, 768], P('expert', 'dp'), may hold values from -0.125 to 0.125
- up_weight: bfloat16 [16, 2048, 768], P('expert', 'dp'), may hold values from -0.125 to 0.125
- down_weight: bfloat16 [16, 2048, 768], P('expert', 'dp'), may hold values from -0.21875 to 0.21875
Outputs:
- moe_out: bfloat16 [65536, 2048], P(('dp', 'expert'))
- in_grad: bfloat16 [65536, 2048], P(('dp', 'expert'))
- grad_gate: float32 [16, 2048, 768], P('expert', 'dp')
- grad_up: float32 [16, 2048, 768], P('expert', 'dp')
- grad_down: float32 [16, 2048, 768], P('expert', 'dp')
Inputs may be any that keep to these rules, and one draw needn't show every extreme that they name: `owner_rows`: each row sums to 4096, and the largest entry of each row is exactly 384. `routes`: within the 256 rows of one device no expert is named by more than 24 rows, and in some devices' rows some expert is named by exactly 24.
All inputs are finite; a program needn't handle non-finite values.
Results may differ from a plain program's by a relative error of at most 0.02.
Values may be sent and summed in bfloat16 or wider, within the bound.
A program may use at most 128 MiB of HBM per device.

v0:
```python
import jax
import jax.numpy as jnp
from jax import lax
from jax.experimental import pallas as pl
from jax.experimental.pallas import tpu as pltpu
from jax.sharding import PartitionSpec as P

MESH = pl.DeviceIdType.MESH
BF = jnp.bfloat16
F32 = jnp.float32
N = 16
Z = 8
CAP = 24
CH = 2 * CAP
HALF = 1024
ROWS = N * CAP
STK = 2 * ROWS
TOK = 256
D = 2048
FF = 768
SH = 128
GATE, UP, DOWN = 0, 1, 2
PLANE = ((2, 2), (1, 3), (3, 1), (1, 1), (3, 3), (2, 1), (1, 2), (2, 3), (3, 2), (2, 0), (0, 2), (1, 0), (0, 1), (3, 0), (0, 3))


def nn(a, b):
    return jnp.dot(a, b, preferred_element_type=F32)


def nt(a, b):
    return lax.dot_general(a, b, (((1,), (1,)), ((), ())), preferred_element_type=F32)


def kernel(
    x_hbm, dy_hbm, lens_hbm, routes_hbm, gates_hbm, wg_hbm, wu_hbm, wd_hbm,
    out_hbm, dx_hbm, gg_hbm, gu_hbm, gd_hbm,
    lens, routes, gates, xin, yin, xs, ys, gotx, goty, s2x, s2y, rcx, rcy, backo, backd,
    w, perm, perm_g, a_t, sel,
    xt, yt, xt_s, yt_s, hid, gcot, ucot, f1, f2, f3, tmp, s4, sb, mo, gr,
    ld, rel_s, rel_r, ex_s, ex_r, bk_s, bk_r, ag_s, ag_r, sib_s, sib_r, act_s, act_r, rs_s, rs_r, st,
):
    dp = lax.axis_index("dp")
    ex = lax.axis_index("expert")
    z = dp // 2
    c = lax.rem(dp, 2)
    sibling = {"dp": dp + 1 - 2 * c}

    bar = pltpu.get_barrier_semaphore()

    def greet(i, _):
        pl.semaphore_signal(bar, 1, device_id={"dp": lax.rem(dp + i, N)}, device_id_type=MESH)
        pl.semaphore_signal(bar, 1, device_id={"expert": lax.rem(ex + i, N)}, device_id_type=MESH)
        return 0

    lax.fori_loop(1, N, greet, 0)

    loads = []
    for i, (src, dst) in enumerate(((x_hbm, xin), (dy_hbm, yin))):
        for h in range(2):
            loads.append(pltpu.make_async_copy(
                src.at[:, pl.ds(h * HALF, HALF)], dst.at[pl.ds(h * ROWS, ROWS)], ld.at[2 * i + h]))
    my_half = pl.ds(pl.multiple_of(c * SH, SH), SH)
    for i, src in enumerate((wg_hbm, wu_hbm, wd_hbm)):
        loads.append(pltpu.make_async_copy(src.at[0], w.at[i, 0, my_half], ld.at[4 + i]))
    for i, (src, dst) in enumerate(((lens_hbm, lens), (routes_hbm, routes), (gates_hbm, gates))):
        loads.append(pltpu.make_async_copy(src, dst, ld.at[7 + i]))
    for cp in loads[4:7] + loads[:4] + loads[7:]:
        cp.start()

    def permute(p_ref, src, dst):
        def body(t, _):
            cols = pl.ds(pl.multiple_of(t * 256, 256), 256)
            dst[:, cols] = nn(p_ref[...], src[:, cols]).astype(BF)
            return 0
        lax.fori_loop(0, HALF // 256, body, 0)

    def tile(i):
        return pl.ds(pl.multiple_of(i * CH, CH), CH)

    def scatter(src, dst, ssem, rsem, axis, me):
        def body(i, _):
            t = lax.rem(me + i, N)
            pltpu.make_async_remote_copy(
                src_ref=src.at[tile(t)], dst_ref=dst.at[tile(me)], send_sem=ssem, recv_sem=rsem,
                device_id={axis: t}, device_id_type=MESH).start()
            return 0
        lax.fori_loop(1, N, body, 0)
        dst[tile(me), :] = src[tile(me), :]

    def spread(src, dst, ssem, rsem):
        row, column = ex // 4, lax.rem(ex, 4)
        for a, b in PLANE:
            t = lax.rem(row + a, 4) * 4 + lax.rem(column + b, 4)
            pltpu.make_async_remote_copy(
                src_ref=src.at[tile(t)], dst_ref=dst.at[tile(ex)], send_sem=ssem, recv_sem=rsem,
                device_id={"expert": t}, device_id_type=MESH).start()
        dst[tile(ex), :] = src[tile(ex), :]

    def scatter_all(src, dst, ssem, rsem, axis):
        me = dp if axis == "dp" else ex
        span = pl.ds(0, (N - 1) * CH)
        return pltpu.make_async_remote_copy(
            src_ref=src.at[span], dst_ref=dst.at[span], send_sem=ssem, recv_sem=rsem,
            device_id={axis: lax.rem(me + 1, N)}, device_id_type=MESH)

    def span_of(hop, way):
        if hop < 4:
            return 0, SH
        return (0 if way == 0 else 64), 64

    def chip(k):
        return lax.rem(z + k + 2 * Z, Z)

    def ag(i, way, hop):
        sign = 1 - 2 * way
        lo, n = span_of(hop, way)
        rows = pl.ds(pl.multiple_of(c * SH + lo, 64), n)
        return pltpu.make_async_remote_copy(
            src_ref=w.at[i, (-sign * (hop - 1)) % Z, rows], dst_ref=w.at[i, (-sign * hop) % Z, rows],
            send_sem=ag_s.at[i, way, hop - 1], recv_sem=ag_r.at[i, way, hop - 1],
            device_id={"dp": 2 * chip(sign) + c}, device_id_type=MESH)

    def share(i, k, hop):
        block = w.at[i, k % Z, my_half]
        return pltpu.make_async_remote_copy(
            src_ref=block, dst_ref=block, send_sem=sib_s.at[i, hop], recv_sem=sib_r.at[i, hop],
            device_id=sibling, device_id_type=MESH)

    def shared(i, hop):
        block = w.at[i, hop, pl.ds(0, SH if hop in (0, 4) else 2 * SH)]
        return pltpu.make_async_remote_copy(
            src_ref=block, dst_ref=block, send_sem=sib_s.at[i, hop], recv_sem=sib_r.at[i, hop],
            device_id=sibling, device_id_type=MESH)

    def ag_step(i, hop):
        for way in range(2):
            ag(i, way, hop).wait_recv()
            if hop < 4:
                ag(i, way, hop + 1).start()
                share(i, (2 * way - 1) * hop, hop).start()
        if hop == 4:
            share(i, 4, 4).start()

    for i in range(3):
        loads[4 + i].wait()
    pl.semaphore_wait(bar, 2 * (N - 1))

    def ag_first(i):
        ag(i, 0, 1).start()
        ag(i, 1, 1).start()
        share(i, 0, 0).start()

    ag_first(GATE)
    ag_first(UP)
    loads[7].wait()
    def prefix(i, acc):
        return acc + jnp.where(i < dp, lens[0, i], 0)

    start = lax.fori_loop(0, N, prefix, jnp.int32(0))
    col = lax.broadcasted_iota(jnp.int32, (1, STK), 1)
    right_half = (col >= ROWS).astype(jnp.int32)
    r = col - ROWS * right_half
    dest = ((r + start) & (N - 1)) * CH + CAP * right_half + (r >> 4)
    row_iota = lax.broadcasted_iota(jnp.int32, (STK, STK), 0)
    perm[...] = jnp.where(row_iota == dest, 1.0, 0.0).astype(BF)

    loads[0].wait()
    loads[1].wait()
    permute(perm, xin, xs)
    scatter(xs, gotx, rel_s.at[0], rel_r.at[0], "dp", dp)
    loads[2].wait()
    loads[3].wait()
    permute(perm, yin, ys)
    scatter(ys, goty, rel_s.at[1], rel_r.at[1], "dp", dp)
    ag_first(DOWN)

    expert_iota = lax.broadcasted_iota(jnp.int32, (N, TOK), 0)
    loads[8].wait()
    loads[9].wait()
    route = routes[...]
    hot = expert_iota == route
    hot_f = jnp.where(hot, 1.0, 0.0)
    earlier = (lax.broadcasted_iota(jnp.int32, (TOK, TOK), 0) < lax.broadcasted_iota(jnp.int32, (TOK, TOK), 1))
    before = nn(hot_f.astype(BF), jnp.where(earlier, 1.0, 0.0).astype(BF))
    rank = jnp.sum(before * hot_f, axis=0, keepdims=True).astype(jnp.int32)
    slot = route * CH + rank
    pos = N * lax.broadcasted_iota(jnp.int32, (1, TOK), 1) + dp
    owner = jnp.zeros((1, TOK), jnp.int32)
    first = jnp.zeros((1, TOK), jnp.int32)
    end = jnp.int32(0)
    for b in range(N):
        end = end + lens[0, b]
        past = pos >= end
        owner = owner + jnp.where(past, 1, 0)
        first = jnp.where(past, end, first)
    got_row = owner * CH + ((pos - first) >> 4)
    gate_f = gates[...].astype(F32).reshape(1, TOK)
    tall = lax.broadcasted_iota(jnp.int32, (STK, TOK), 0)
    eye = jnp.where(
        lax.broadcasted_iota(jnp.int32, (TOK, TOK), 0) == lax.broadcasted_iota(jnp.int32, (TOK, TOK), 1), 1.0, 0.0
    ).astype(BF)
    for h in range(2):
        cols = pl.ds(h * TOK, TOK)
        hit = tall == slot + h * CAP
        plain = jnp.where(hit, 1.0, 0.0).astype(BF)
        gated = jnp.where(hit, gate_f, 0.0).astype(BF)
        a_t[0, :, cols] = plain
        a_t[1, :, cols] = gated
        a_t[2, :, cols] = jnp.where(tall == got_row + h * CAP, 1.0, 0.0).astype(BF)
        sel[0, h] = nt(eye, gated).astype(BF)
        sel[1, h] = nt(eye, plain).astype(BF)

    def build(t, _):
        rows = pl.ds(pl.multiple_of(t * 256, 256), 256)
        perm[rows, :] = nt(a_t[0, rows, :], a_t[2]).astype(BF)
        perm_g[rows, :] = nt(a_t[1, rows, :], a_t[2]).astype(BF)
        return 0

    lax.fori_loop(0, STK // 256, build, 0)

    def unstack(src, dst):
        def body(t, _):
            one = src[tile(2 * t), :].astype(F32)
            two = src[tile(2 * t + 1), :].astype(F32)
            at = pl.multiple_of(t * CH, CH)
            dst[pl.ds(at, CH), :] = jnp.concatenate([one[:CAP], two[:CAP]], axis=0).astype(BF)
            dst[pl.ds(at + ROWS, CH), :] = jnp.concatenate([one[CAP:], two[CAP:]], axis=0).astype(BF)
            return 0
        lax.fori_loop(0, N // 2, body, 0)

    own_rows = pl.ds(pl.multiple_of(c * ROWS, ROWS), ROWS)
    eye_s = eye[:SH, :SH]

    def turn(src, mine, theirs):
        def body(t, _):
            for par, dst in ((c, None), (1 - c, theirs)):
                d = 2 * t + par
                block = src[pl.ds(pl.multiple_of((d // Z) * ROWS, ROWS), ROWS),
                            pl.ds(pl.multiple_of(lax.rem(d, Z) * SH, SH), SH)]
                turned = nt(eye_s, block).astype(BF)
                if dst is None:
                    mine[t, :, own_rows] = turned
                else:
                    dst[t] = turned
            return 0
        lax.fori_loop(0, Z, body, 0)

    def give(i, src, dst):
        return pltpu.make_async_remote_copy(
            src_ref=src, dst_ref=dst, send_sem=act_s.at[i], recv_sem=act_r.at[i],
            device_id=sibling, device_id_type=MESH)

    gifts = (
        give(0, xt_s, xt.at[:, :, own_rows]),
        give(1, yt_s, yt.at[:, :, own_rows]),
        give(2, hid.at[own_rows], hid.at[own_rows]),
        give(3, gcot.at[own_rows], gcot.at[own_rows]),
        give(4, ucot.at[own_rows], ucot.at[own_rows]),
    )

    ag_step(GATE, 1)
    ag_step(UP, 1)
    scatter_all(xs, gotx, rel_s.at[0], rel_r.at[0], "dp").wait_recv()
    permute(perm, gotx, s2x)
    spread(s2x, rcx, ex_s.at[0], ex_r.at[0])
    scatter_all(ys, goty, rel_s.at[1], rel_r.at[1], "dp").wait_recv()
    permute(perm_g, goty, s2y)
    spread(s2y, rcy, ex_s.at[1], ex_r.at[1])
    ag_step(GATE, 2)
    scatter_all(s2x, rcx, ex_s.at[0], ex_r.at[0], "expert").wait_recv()
    unstack(rcx, xin)
    turn(xin, xt, xt_s)
    gifts[0].start()
    ag_step(UP, 2)
    ag_step(DOWN, 1)

    def chip_product(src, i, k, cols):
        o = chip(k)
        rows = src[pl.ds(pl.multiple_of((o // 4) * ROWS, ROWS), ROWS), pl.ds(pl.multiple_of(lax.rem(o, 4) * 256, 256), 256)]
        return nn(rows, w[i, k % Z, :, cols])

    def part(i, src, acc, hops):
        steps = []
        for hop in hops:
            shared(i, hop).wait_recv()
            steps += [hop] if hop in (0, 4) else [hop, -hop]
        for t in range(FF // 256):
            cols = pl.ds(t * 256, 256)
            total = chip_product(src, i, steps[0], cols)
            for k in steps[1:]:
                total = total + chip_product(src, i, k, cols)
            acc[:, cols] = total if 0 in hops else acc[:, cols] + total

    part(GATE, xin, f1, (0, 1))
    part(UP, xin, f2, (0, 1))
    ag_step(GATE, 3)
    part(GATE, xin, f1, (2,))
    part(UP, xin, f2, (2,))
    ag_step(UP, 3)
    scatter_all(s2y, rcy, ex_s.at[1], ex_r.at[1], "expert").wait_recv()
    unstack(rcy, yin)
    turn(yin, yt, yt_s)
    gifts[1].start()
    ag_step(DOWN, 2)
    part(GATE, xin, f1, (3,))
    part(UP, xin, f2, (3,))
    part(DOWN, yin, f3, (0, 1))
    ag_step(GATE, 4)
    ag_step(UP, 4)
    part(DOWN, yin, f3, (2,))
    shared(GATE, 4).wait_recv()
    shared(UP, 4).wait_recv()

    def forward(t, _):
        cols = pl.ds(pl.multiple_of(t * 256, 256), 256)
        g = f1[:, cols] + chip_product(xin, GATE, 4, cols)
        u = f2[:, cols] + chip_product(xin, UP, 4, cols)
        sg = jax.nn.sigmoid(g)
        active = g * sg
        hid[own_rows, cols] = (active * u).astype(BF)
        f1[:, cols] = u * sg * (1.0 + g * (1.0 - sg))
        f2[:, cols] = active
        return 0

    lax.fori_loop(0, FF // 256, forward, 0)
    gifts[2].start()
    ag_step(DOWN, 3)

    def rs(i, way, hop):
        sign = 1 - 2 * way
        lo, n = span_of(hop, way)
        rows = pl.ds(lo, n)
        src = s4.at[i, rows] if hop == 4 else sb.at[i, way, hop, rows]
        return pltpu.make_async_remote_copy(
            src_ref=src, dst_ref=sb.at[i, way, hop - 1, rows], send_sem=rs_s.at[i, way, hop - 1],
            recv_sem=rs_r.at[i, way, hop - 1], device_id={"dp": 2 * chip(sign) + c}, device_id_type=MESH)

    def term(i, k):
        left = yt if i == DOWN else xt
        right = (gcot, ucot, hid)[i]
        return nn(left[chip(k)], right[...])

    def rs_own(i, hop):
        if hop == 4:
            s4[i] = term(i, 4).astype(BF)
        elif hop == 0:
            tmp[0] = term(i, 0)
        else:
            tmp[0] = term(i, hop)
            tmp[1] = term(i, -hop)

    def rs_pass(i, hop):
        if hop == 4:
            rs(i, 0, 4).start()
            rs(i, 1, 4).start()
            return
        if hop == 0:
            for way in range(2):
                rs(i, way, 1).wait_recv()
            gr[i] = tmp[0] + sb[i, 0, 0].astype(F32) + sb[i, 1, 0].astype(F32)
            return
        for way in range(2):
            lo, n = span_of(hop + 1, way)
            rs(i, way, hop + 1).wait_recv()
            sb[i, way, hop, pl.ds(lo, n)] = (
                tmp[way, pl.ds(lo, n)] + sb[i, way, hop, pl.ds(lo, n)].astype(F32)).astype(BF)
            if n < SH:
                sb[i, way, hop, pl.ds(64 - lo, 64)] = tmp[way, pl.ds(64 - lo, 64)].astype(BF)
            rs(i, way, hop).start()

    def rs_step(i, hop):
        rs_own(i, hop)
        rs_pass(i, hop)

    gifts[1].wait_recv()
    gifts[2].wait_recv()
    rs_step(DOWN, 4)
    part(DOWN, yin, f3, (3,))

    def restack(first, second, dst, cols):
        for e in range(N):
            rows = slice(e * CAP, (e + 1) * CAP)
            dst[pl.ds(e * CH, CH), cols] = jnp.concatenate([first[rows], second[rows]], axis=0).astype(BF)

    def produce(k):
        left = hid[own_rows, :]
        restack(nt(left, w[DOWN, k]), nt(left, w[DOWN, k + 4]), xs, pl.ds(k * 256, 256))

    scatter_all(xs, gotx, rel_s.at[0], rel_r.at[0], "dp").wait_send()
    scatter_all(ys, goty, rel_s.at[1], rel_r.at[1], "dp").wait_send()
    rs_own(DOWN, 3)
    produce(1)
    ag_step(DOWN, 4)
    rs_pass(DOWN, 3)
    produce(2)
    shared(DOWN, 4).wait_recv()

    def backward(t, _):
        cols = pl.ds(pl.multiple_of(t * 256, 256), 256)
        hc = f3[:, cols] + chip_product(yin, DOWN, 4, cols)
        gcot[own_rows, cols] = (hc * f1[:, cols]).astype(BF)
        ucot[own_rows, cols] = (hc * f2[:, cols]).astype(BF)
        return 0

    lax.fori_loop(0, FF // 256, backward, 0)
    gifts[3].start()
    gifts[4].start()
    produce(3)
    produce(0)
    spread(xs, backo, bk_s.at[0], bk_r.at[0])
    gifts[0].wait_recv()
    gifts[3].wait_recv()
    rs_step(GATE, 4)
    gifts[4].wait_recv()
    rs_step(UP, 4)
    rs_step(DOWN, 2)

    def cotangent(k, _):
        lg, lu = gcot[own_rows, :], ucot[own_rows, :]
        parts = [nt(lg, w[GATE, k + 4 * h]) + nt(lu, w[UP, k + 4 * h]) for h in range(2)]
        restack(parts[0], parts[1], ys, pl.ds(pl.multiple_of(k * 256, 256), 256))
        return 0

    lax.fori_loop(0, HALF // 256, cotangent, 0)
    spread(ys, backd, bk_s.at[1], bk_r.at[1])

    stores = []

    def finish(i):
        rs_step(i, 0)
        cp = pltpu.make_async_copy(gr.at[i], (gg_hbm, gu_hbm, gd_hbm)[i].at[0], st.at[2 + i])
        cp.start()
        stores.append(cp)

    rs_step(GATE, 3)
    rs_step(UP, 3)
    rs_step(DOWN, 1)
    rs_step(GATE, 2)
    rs_step(UP, 2)
    finish(DOWN)

    def collect(i, src, dst):
        def body(t, _):
            cols = pl.ds(pl.multiple_of(t * 256, 256), 256)
            for h in range(2):
                at = pl.multiple_of(lax.rem(z + t + 4 * h, Z) * 256, 256)
                mo[i, :, pl.ds(at, 256)] = nn(sel[i, h], src[:, cols]).astype(BF)
            return 0
        lax.fori_loop(0, HALF // 256, body, 0)
        cp = pltpu.make_async_copy(mo.at[i], dst, st.at[i])
        cp.start()
        return cp

    scatter_all(xs, backo, bk_s.at[0], bk_r.at[0], "expert").wait_recv()
    stores.append(collect(0, backo, out_hbm))
    rs_step(GATE, 1)
    rs_step(UP, 1)
    finish(GATE)
    scatter_all(ys, backd, bk_s.at[1], bk_r.at[1], "expert").wait_recv()
    stores.append(collect(1, backd, dx_hbm))

    scatter_all(s2x, rcx, ex_s.at[0], ex_r.at[0], "expert").wait_send()
    scatter_all(s2y, rcy, ex_s.at[1], ex_r.at[1], "expert").wait_send()
    scatter_all(xs, backo, bk_s.at[0], bk_r.at[0], "expert").wait_send()
    scatter_all(ys, backd, bk_s.at[1], bk_r.at[1], "expert").wait_send()
    for g in gifts:
        g.wait_send()
    for i in range(3):
        for hop in range(5):
            shared(i, hop).wait_send()
        for way in range(2):
            for hop in range(1, 5):
                ag(i, way, hop).wait_send()
            for hop in range(2, 5):
                rs(i, way, hop).wait_send()
    finish(UP)
    for i in range(3):
        for way in range(2):
            rs(i, way, 1).wait_send()
    for cp in stores:
        cp.wait()


def hand_over(*refs):
    src, dst, held, sems = refs[:5], refs[5:10], refs[10:15], refs[15]
    pieces = [(i, pl.ds(r, 64)) for r in range(0, TOK, 64) for i in range(2)]
    pieces += [(i, pl.ds(0, 1)) for i in range(2, 5)]
    reads = [pltpu.make_async_copy(src[i].at[r], held[i].at[r], sems.at[0, n]) for n, (i, r) in enumerate(pieces)]
    writes = [pltpu.make_async_copy(held[i].at[r], dst[i].at[r], sems.at[1, n]) for n, (i, r) in enumerate(pieces)]
    for cp in reads:
        cp.start()
    for read, write in zip(reads, writes):
        read.wait()
        write.start()
    for cp in writes:
        cp.wait()


def local(attn_rows, out_grad, owner_rows, routes, gates, gate_weight, up_weight, down_weight):
    any_ = pl.BlockSpec(memory_space=pl.ANY)
    V, S = pltpu.VMEM, pltpu.SemaphoreType.DMA
    rows_t = V((STK, HALF), BF)
    scratch = [pltpu.SMEM((1, N), jnp.int32), V((1, TOK), jnp.int32), V((TOK,), BF)] + [rows_t] * 12 + [
        V((3, Z, 2 * SH, FF), BF), V((STK, STK), BF), V((STK, STK), BF), V((3, STK, 2 * TOK), BF), V((2, 2, TOK, STK), BF),
        V((Z, SH, STK), BF), V((Z, SH, STK), BF), V((Z, SH, ROWS), BF), V((Z, SH, ROWS), BF),
        V((STK, FF), BF), V((STK, FF), BF), V((STK, FF), BF), V((ROWS, FF), F32), V((ROWS, FF), F32), V((ROWS, FF), F32),
        V((2, SH, FF), F32), V((3, SH, FF), BF), V((3, 2, 4, SH, FF), BF), V((2, TOK, D), BF), V((3, SH, FF), F32),
        S((10,)), S((2,)), S((2,)), S((2,)), S((2,)), S((2,)), S((2,)), S((3, 2, 4)), S((3, 2, 4)), S((3, 5)), S((3, 5)),
        S((5,)), S((5,)), S((3, 2, 4)), S((3, 2, 4)), S((5,)),
    ]
    grad = jax.ShapeDtypeStruct((1, SH, FF), F32)
    rows_o = jax.ShapeDtypeStruct((TOK, D), BF)
    results = pl.pallas_call(
        kernel,
        out_shape=(rows_o, rows_o, grad, grad, grad),
        in_specs=[any_] * 8,
        out_specs=(any_,) * 5,
        scratch_shapes=scratch,
        compiler_params=pltpu.CompilerParams(collective_id=0, has_side_effects=True, vmem_limit_bytes=63 << 20),
        cost_estimate=pl.CostEstimate(flops=20_000_000_000, bytes_accessed=12_000_000, transcendentals=300_000),
    )(attn_rows, out_grad, owner_rows, routes.reshape(1, TOK), gates,
      gate_weight, up_weight, down_weight)
    return pl.pallas_call(
        hand_over,
        out_shape=(rows_o, rows_o, grad, grad, grad),
        in_specs=[any_] * 5,
        out_specs=(any_,) * 5,
        scratch_shapes=[V((TOK, D), BF), V((TOK, D), BF)] + [V((1, SH, FF), F32)] * 3 + [S((2, 11))],
    )(*results)


def solution(mesh):
    in_specs = (
        P(("dp", "expert"), None),
        P(("dp", "expert"), None),
        P("expert", None),
        P(("dp", "expert"), None),
        P(("dp", "expert")),
        P("expert", "dp", None),
        P("expert", "dp", None),
        P("expert", "dp", None),
    )
    out_specs = (
        P(("dp", "expert"), None),
        P(("dp", "expert"), None),
        P("expert", "dp", None),
        P("expert", "dp", None),
        P("expert", "dp", None),
    )
    return jax.shard_map(local, mesh=mesh, in_specs=in_specs, out_specs=out_specs, check_vma=False)
```

profile of v0, /device:TPU:1, one launch (start us, length us, event | category | flops | bytes accessed | tf_op | source)
XLA Modules:
  0.0 178.8 jit_solution(1603117181701005658)
XLA Ops:
  0.6 175.1 %shard_map.119 = (bf16[256,2048]{1,0:T(8,128)(2,1)}, bf16[256,2048]{1,0:T(8,128)(2,1)}, f32[1,128,768]{2,1,0:T(8,128)}, f32[1,128,768]{2,1,0:T(8,128)}, f32[1,128,768]{2,1,0:T(8,128)}) custom-call(bf16[384,2048]{1,0:T(8,128)(2,1)} %x_hbm.1, bf16[384,2048]{1,0:T(8,128)(2,1)} %dy_hbm.1, s32[1,16]{1,0:T(1,128)} %lens_hbm.1, s32[1,256]{1,0:T(1,128)} %bitcast.1, ...), custom_call_target="tpu_custom_call" | custom-call | flops 20000000000 | bytes 12000000 | tf_op jit(solution)/shard_map/pallas_call | solution.py:513
  175.8 2.9 %shard_map.120 = (bf16[256,2048]{1,0:T(8,128)(2,1)}, bf16[256,2048]{1,0:T(8,128)(2,1)}, f32[1,128,768]{2,1,0:T(8,128)}, f32[1,128,768]{2,1,0:T(8,128)}, f32[1,128,768]{2,1,0:T(8,128)}) custom-call(bf16[256,2048]{1,0:T(8,128)(2,1)} %get-tuple-element.10.refs_0_, bf16[256,2048]{1,0:T(8,128)(2,1)} %get-tuple-element.11.refs_1_, ...), custom_call_target="tpu_custom_call" | custom-call | tf_op jit(solution)/shard_map/pallas_call | solution.py:523
where the time goes:
time: 179 us
  Pallas kernels  178 us (99%)
    pallas_call x1, Pallas kernels, local(): pl.pallas_call(kernel, out_shape=(rows_o, rows_o, grad, grad, grad), in_s...  175 us

commit v1 on v0

--- a/solution.py
+++ b/solution.py
@@ -312,7 +312,7 @@
     shared(UP, 4).wait_recv()
 
     def forward(t, _):
-        cols = pl.ds(pl.multiple_of(t * 256, 256), 256)
+        cols = pl.ds(t * 256, 256)
         g = f1[:, cols] + chip_product(xin, GATE, 4, cols)
         u = f2[:, cols] + chip_product(xin, UP, 4, cols)
         sg = jax.nn.sigmoid(g)
@@ -320,10 +320,11 @@
         hid[own_rows, cols] = (active * u).astype(BF)
         f1[:, cols] = u * sg * (1.0 + g * (1.0 - sg))
         f2[:, cols] = active
+        give(2, hid.at[own_rows, cols], hid.at[own_rows, cols]).start()
         return 0
 
-    lax.fori_loop(0, FF // 256, forward, 0)
-    gifts[2].start()
+    for t in range(FF // 256):
+        forward(t, 0)
     ag_step(DOWN, 3)
 
     def rs(i, way, hop):
@@ -396,15 +397,16 @@
     shared(DOWN, 4).wait_recv()
 
     def backward(t, _):
-        cols = pl.ds(pl.multiple_of(t * 256, 256), 256)
+        cols = pl.ds(t * 256, 256)
         hc = f3[:, cols] + chip_product(yin, DOWN, 4, cols)
         gcot[own_rows, cols] = (hc * f1[:, cols]).astype(BF)
         ucot[own_rows, cols] = (hc * f2[:, cols]).astype(BF)
+        give(3, gcot.at[own_rows, cols], gcot.at[own_rows, cols]).start()
+        give(4, ucot.at[own_rows, cols], ucot.at[own_rows, cols]).start()
         return 0
 
-    lax.fori_loop(0, FF // 256, backward, 0)
-    gifts[3].start()
-    gifts[4].start()
+    for t in range(FF // 256):
+        backward(t, 0)
     produce(3)
     produce(0)
     spread(xs, backo, bk_s.at[0], bk_r.at[0])
@@ -421,7 +423,9 @@
         restack(parts[0], parts[1], ys, pl.ds(pl.multiple_of(k * 256, 256), 256))
         return 0
 
-    lax.fori_loop(0, HALF // 256, cotangent, 0)
+    lax.fori_loop(0, 2, cotangent, 0)
+    rs_step(GATE, 3)
+    lax.fori_loop(2, HALF // 256, cotangent, 0)
     spread(ys, backd, bk_s.at[1], bk_r.at[1])
 
     stores = []
@@ -432,7 +436,6 @@
         cp.start()
         stores.append(cp)
 
-    rs_step(GATE, 3)
     rs_step(UP, 3)
     rs_step(DOWN, 1)
     rs_step(GATE, 2)

time: 179 us -> 179 us (level)
  no operation moved by 1% of the time
where the time goes in v1:
time: 179 us
  Pallas kernels  178 us (99%)
    pallas_call x1, Pallas kernels, local(): pl.pallas_call(kernel, out_shape=(rows_o, rows_o, grad, grad, grad), in_s...  175 us

profile of v1, /device:TPU:1, one launch (start us, length us, event | category | flops | bytes accessed | tf_op | source)
XLA Modules:
  0.0 178.9 jit_solution(18353733882734357318)
XLA Ops:
  0.6 175.3 %shard_map.119 = (bf16[256,2048]{1,0:T(8,128)(2,1)}, bf16[256,2048]{1,0:T(8,128)(2,1)}, f32[1,128,768]{2,1,0:T(8,128)}, f32[1,128,768]{2,1,0:T(8,128)}, f32[1,128,768]{2,1,0:T(8,128)}) custom-call(bf16[384,2048]{1,0:T(8,128)(2,1)} %x_hbm.1, bf16[384,2048]{1,0:T(8,128)(2,1)} %dy_hbm.1, s32[1,16]{1,0:T(1,128)} %lens_hbm.1, s32[1,256]{1,0:T(1,128)} %bitcast.1, ...), custom_call_target="tpu_custom_call" | custom-call | flops 20000000000 | bytes 12000000 | tf_op jit(solution)/shard_map/pallas_call | solution.py:516
  175.9 2.9 %shard_map.120 = (bf16[256,2048]{1,0:T(8,128)(2,1)}, bf16[256,2048]{1,0:T(8,128)(2,1)}, f32[1,128,768]{2,1,0:T(8,128)}, f32[1,128,768]{2,1,0:T(8,128)}, f32[1,128,768]{2,1,0:T(8,128)}) custom-call(bf16[256,2048]{1,0:T(8,128)(2,1)} %get-tuple-element.10.refs_0_, bf16[256,2048]{1,0:T(8,128)(2,1)} %get-tuple-element.11.refs_1_, ...), custom_call_target="tpu_custom_call" | custom-call | tf_op jit(solution)/shard_map/pallas_call | solution.py:526
